TPU v7x, 128 devices: a whole 4x4x4 slice. The times are simulated.
128 devices in a mesh: rep: 16 (over x, z_hi, core), fsdp: 8 (over z_lo, y).
Axes of the slice: x: 4, y: 4, z: 4 (z_hi: 2, z_lo: 2; z = z_hi * 2 + z_lo), core: 2. Of those that a mesh axis runs over, the one named last changes fastest.
Arguments:
- tokens: bfloat16 [32768, 12288], P(('rep', 'fsdp')), may hold values from -36 to 36
- norm_gain: bfloat16 [12288], replicated, may hold values from 0.099609375 to 1.8984375
- key_weight: bfloat16 [12288, 1024], P('fsdp'), may hold values from -0.0546875 to 0.0546875
- cotangent: bfloat16 [32768, 1024], P(('rep', 'fsdp')), may hold values from -6 to 6
- outer_deltas: bfloat16 [16, 12288, 1024], P('rep', 'fsdp'), may hold values from -6 to 6
- anchor: float32 [12288, 1024], P('fsdp', 'rep'), may hold values from -6 to 6
- momentum: float32 [12288, 1024], P('fsdp', 'rep'), may hold values from -2 to 2
Outputs:
- keys: bfloat16 [32768, 1024], P(('rep', 'fsdp'))
- token_grad: bfloat16 [32768, 12288], P(('rep', 'fsdp'))
- weight_grad: bfloat16 [16, 12288, 1024], P('rep', 'fsdp')
- new_anchor: float32 [12288, 1024], P('fsdp', 'rep')
- new_momentum: float32 [12288, 1024], P('fsdp', 'rep')
All inputs are finite; a program needn't handle non-finite values.
Results may differ from a plain program's by a relative error of at most 0.019.
Values may be sent and summed in bfloat16 or wider, within the bound.
A program may use at most 192 MiB of HBM per device.

v0:
```python
import jax
import jax.numpy as jnp
from jax import lax
from jax.sharding import PartitionSpec as P

EPS = 1e-05
OUTER_LR = 0.7
OUTER_MU = 0.9


def on_device(tokens, norm_gain, key_weight, cotangent, outer_deltas, anchor, momentum):
    tok_f = tokens.astype(jnp.float32)
    inv_rms = lax.rsqrt(jnp.mean(tok_f * tok_f, axis=1, keepdims=True) + EPS)
    gain_f = norm_gain.astype(jnp.float32)
    normed = (tok_f * inv_rms * gain_f).astype(jnp.bfloat16)
    shard_rows = lax.all_gather(key_weight, "fsdp", axis=0, tiled=True)
    normed_slab = normed
    key_sum = jnp.dot(normed_slab, shard_rows, preferred_element_type=jnp.float32)
    back_part = lax.dot_general(
        cotangent, shard_rows, (((1,), (1,)), ((), ())), preferred_element_type=jnp.float32
    )
    back_grad = back_part
    key_sum, back_grad = (key_sum, back_grad)
    keys = key_sum.astype(jnp.bfloat16)
    upstream = back_grad * gain_f
    inner_mean = jnp.mean(upstream * tok_f, axis=1, keepdims=True)
    token_grad = (inv_rms * upstream - tok_f * inv_rms**3 * inner_mean).astype(jnp.bfloat16)
    normed_slab = normed
    weight_sum = lax.psum_scatter(
        lax.dot_general(
            normed_slab, cotangent, (((0,), (0,)), ((), ())), preferred_element_type=jnp.float32
        ).astype(jnp.bfloat16),
        "fsdp",
        scatter_dimension=0,
        tiled=True,
    )
    weight_grad = weight_sum[None]
    delta_terms = outer_deltas[0].astype(jnp.float32)
    share_cols = anchor.shape[1]
    delta_total = lax.psum(delta_terms.astype(jnp.bfloat16), "rep").astype(jnp.float32)
    delta_share = lax.dynamic_slice_in_dim(
        delta_total, lax.axis_index("rep") * share_cols, share_cols, 1
    )
    mean_delta = delta_share / lax.axis_size("rep")
    new_momentum = OUTER_MU * momentum + mean_delta
    new_anchor = anchor - OUTER_LR * (mean_delta + OUTER_MU * new_momentum)
    return (keys, token_grad, weight_grad, new_anchor, new_momentum)


def solution(mesh):
    return jax.shard_map(
        on_device,
        mesh=mesh,
        in_specs=(
            P(("rep", "fsdp"), None),
            P(),
            P("fsdp", None),
            P(("rep", "fsdp"), None),
            P("rep", "fsdp", None),
            P("fsdp", "rep"),
            P("fsdp", "rep"),
        ),
        out_specs=(
            P(("rep", "fsdp"), None),
            P(("rep", "fsdp"), None),
            P("rep", "fsdp", None),
            P("fsdp", "rep"),
            P("fsdp", "rep"),
        ),
        check_vma=False,
    )
```

profile of v0, /device:TPU:1, one launch (start us, length us, event | category | flops | bytes accessed | tf_op | source)
XLA Modules:
  0.0 660.2 jit_solution(2637531356927620455)
XLA Ops:
  8.0 0.0 copy-start
  8.0 0.0 copy-start.4
  8.0 0.0 all-gather.2.cloned.1.call-start
  8.1 0.7 all-gather.2.cloned.1.call-update
  8.8 0.0 all-reduce.2.cloned.1.call-start
  8.8 4.6 copy.12
  13.4 0.0 all-reduce.2.cloned.1.call-update
  13.5 0.0 reduce-scatter.2.cloned.1.call-start
  13.5 0.0 copy-done.4
  13.5 251.6 %all-gather.2.cloned.1.call-done = bf16[12288,1024]{1,0:T(8,128)(2,1)} async-done(((bf16[1536,1024]{1,0:T(8,128)(2,1)}), bf16[12288,1024]{1,0:T(8,128)(2,1)}) %all-gather.2.cloned.1.call-update) | async-done | bytes 25165840 | tf_op jit(solution)/shard_map/all_gather | solution.py:16
  265.2 0.0 copy-done
  265.2 18.4 %fusion.6 = (f32[256]{0:T(256)S(1)}, f32[256]{0:T(256)S(1)}, f32[256,12288]{1,0:T(8,128)}) fusion(bf16[256,12288]{1,0:T(8,128)(2,1)} %param.7, f32[12288]{0:T(1024)S(1)} %convert_element_type.24, bf16[256,1024]{1,0:T(8,128)(2,1)S(1)} %copy-done, bf16[12288,1024]{1,0:T(8,128)(2,1)} %all-gather.2.cloned.1.call-done), kind=kOutput, calls=%fused_computation.12 | convolution fusion | flops 6461325312 | bytes 44615680 | tf_op jit(solution)/shard_map/dot_general | solution.py:19
  283.5 15.4 %convolution_convert_fusion = bf16[12288,1024]{1,0:T(8,128)(2,1)} fusion(bf16[256,1024]{1,0:T(8,128)(2,1)S(1)} %copy-done, bf16[256,12288]{1,0:T(8,128)(2,1)} %param.7, f32[12288]{0:T(1024)S(1)} %convert_element_type.24, f32[256]{0:T(256)S(1)} %get-tuple-element.10), kind=kOutput, calls=%fused_computation | convolution fusion | flops 6467616768 | bytes 32031744 | tf_op jit(solution)/shard_map/dot_general | solution.py:30
  298.9 0.0 copy-start.2
  298.9 0.0 copy-start.3
  298.9 0.0 slice-start
  298.9 0.0 reduce-scatter.2.cloned.1.call-update
  299.0 327.8 %all-reduce.2.cloned.1.call-done = bf16[1536,1024]{0,1:T(8,128)(2,1)} async-done(((bf16[1536,1024]{0,1:T(8,128)(2,1)}), bf16[1536,1024]{0,1:T(8,128)(2,1)}) %all-reduce.2.cloned.1.call-update) | async-done | bytes 3145744 | tf_op jit(solution)/shard_map/psum | solution.py:40
  626.7 0.0 copy-done.2
  626.8 0.0 copy-done.3
  626.8 1.9 multiply_subtract_fusion
  628.7 0.0 slice-start.1
  628.7 14.3 %fusion.10 = bf16[256,1024]{1,0:T(8,128)(2,1)} fusion(bf16[12288,1024]{1,0:T(8,128)(2,1)} %all-gather.2.cloned.1.call-done, bf16[256,12288]{1,0:T(8,128)(2,1)} %param.7, f32[12288]{0:T(1024)S(1)} %convert_element_type.24, f32[256]{0:T(256)S(1)} %get-tuple-element.10), kind=kOutput, calls=%fused_computation.14 | convolution fusion | flops 6455296000 | bytes 32031744 | tf_op jit(solution)/shard_map/dot_general | solution.py:18
  642.9 0.0 copy-start.1
  642.9 0.0 slice-done
  642.9 0.0 slice-done.1
  643.0 9.8 %fusion.5 = bf16[256,12288]{1,0:T(8,128)(2,1)} fusion(bf16[256,12288]{1,0:T(8,128)(2,1)S(1)} %bitcast.7, f32[256,12288]{1,0:T(8,128)} %get-tuple-element.11, f32[256]{0:T(256)S(1)} %broadcast_multiply_fusion, f32[256]{0:T(256)S(1)} %get-tuple-element.9, f32[256]{0:T(256)S(1)} %get-tuple-element.10), kind=kLoop, calls=%fused_computation.11 | loop fusion | flops 18874368 | bytes 25168896 | tf_op jit(solution)/shard_map/convert_element_type | solution.py:27
  652.8 0.0 reduce-scatter.2.cloned.1.call-done
  652.8 0.0 copy-done.1
  (4 shorter events, 0.0 us)
Async XLA Ops:
  8.0 257.2 %copy-start = (bf16[256,1024]{1,0:T(8,128)(2,1)S(1)}, bf16[256,1024]{1,0:T(8,128)(2,1)}, u32[]{:S(2)}) copy-start(bf16[256,1024]{1,0:T(8,128)(2,1)} %param.10) | copy-start | bytes 1572868
  8.0 5.5 copy-start.4
  8.0 257.1 %all-gather.2.cloned.1.call-start = ((), (), s32[]{:S(2)}) async-start(), calls=%async_computation.1 | async-start | bytes 28311552 | tf_op jit(solution)/shard_map/all_gather | solution.py:16
  8.8 618.0 %all-reduce.2.cloned.1.call-start = ((), (), s32[]{:S(2)}) async-start(), calls=%async_computation.3 | async-start | bytes 6291456 | tf_op jit(solution)/shard_map/psum | solution.py:40
  13.5 639.3 %reduce-scatter.2.cloned.1.call-start = ((), (), s32[]{:S(2)}) async-start(), calls=%async_computation.2 | async-start | bytes 28311552 | tf_op jit(solution)/shard_map/reduce_scatter | solution.py:29
  298.9 327.8 %copy-start.2 = (f32[1536,64]{0,1:T(8,128)S(1)}, f32[1536,64]{0,1:T(8,128)}, u32[]{:S(2)}) copy-start(f32[1536,64]{0,1:T(8,128)} %param.12) | copy-start | bytes 1179652
  298.9 327.8 %copy-start.3 = (f32[1536,64]{0,1:T(8,128)S(1)}, f32[1536,64]{0,1:T(8,128)}, u32[]{:S(2)}) copy-start(f32[1536,64]{0,1:T(8,128)} %param.13) | copy-start | bytes 1179652
  298.9 344.0 %slice-start = ((s8[6291456]{0:T(1024)(128)(4,1)}), s8[2097152]{0:T(1024)(128)(4,1)S(1)}, s32[]{:S(2)}) async-start(s8[6291456]{0:T(1024)(128)(4,1)} %bitcast.6), calls=%async_computation.4 | async-start | bytes 4194304
  628.7 14.3 %slice-start.1 = ((s8[6291456]{0:T(1024)(128)(4,1)}), s8[4194304]{0:T(1024)(128)(4,1)S(1)}, s32[]{:S(2)}) async-start(s8[6291456]{0:T(1024)(128)(4,1)} %bitcast.6), calls=%async_computation.5 | async-start | bytes 8388608
  642.9 9.9 %copy-start.1 = (bf16[256,1024]{1,0:T(8,128)(2,1)S(1)}, bf16[256,1024]{1,0:T(8,128)(2,1)}, u32[]{:S(2)}) copy-start(bf16[256,1024]{1,0:T(8,128)(2,1)} %param.10) | copy-start | bytes 1572868
Sparse Core Ops, SparseCore 0:
  10.5 254.6 all-gather.1
  299.1 251.0 reduce-scatter.1
Sparse Core Ops, SparseCore 1:
  13.6 613.1 all-reduce.1
where the time goes:
time: 661 us; the launch traced here: 660 us
  waiting for transfers between devices  580 us (88%)
  matrix products  48 us (7%)
  between operations  15.5 us (2%)
  other arithmetic  11.8 us (2%)
    psum x1, waiting for transfers between devices, on_device(): lax.psum(delta_terms.astype(jnp.bfloat16), 'rep').astype(jnp.float32)  328 us
    all_gather x1, waiting for transfers between devices, on_device(): shard_rows = lax.all_gather(key_weight, 'fsdp', axis=0, tiled=True)  252 us
    dot_general x1, matrix products, on_device(): lax.dot_general(cotangent, shard_rows, (((1,), (1,)), ((), ())), preferre...  18.4 us
    dot_general x1, matrix products, on_device(): lax.dot_general(normed_slab, cotangent, (((0,), (0,)), ((), ())), preferr...  15.4 us
    dot_general x1, matrix products, on_device(): jnp.dot(normed_slab, shard_rows, preferred_element_type=jnp.float32)  14.3 us
  transfers between devices with their start and end apart: 3, of which 2 were waited for; matrix products, arithmetic and copies ran while one was open for 10% of the time, Pallas kernels for 0%

commit v1 on v0

v1 whole, which is shorter than its diff:
```python
import functools

import jax
import jax.numpy as jnp
from jax import lax
from jax.experimental import pallas as pl
from jax.experimental.pallas import tpu as pltpu
from jax.sharding import PartitionSpec as P

EPS = 1e-05
OUTER_LR = 0.7
OUTER_MU = 0.9

TOK = 256
D = 12288
KW = 1024
SHARD = 1536
PIECE = 96
CH = 384
HALF = 768

A0 = 0
B0 = 4
X0 = 8
F0 = 16
D0 = 24
T0 = 44
C0 = 52
E0 = 56
G0 = 64
NCH = 65

SPAN = ((1, 4), (0, 4), (1, 4), (0, 4))
FWD_P = ((1, 3), (0, 2), (1, 2), (0, 2))
FWD_M = ((3, 4), (2, 4), (2, 4), (2, 4))


def kernel(
    tok_hbm, gain_ref, kw, cot_hbm, deltas,
    keys_ref, tg_hbm, wg_ref, dsum_ref, wr,
    tok, normed, u, slab, cot, acc, kacc, gainf, inv, rowacc, wbuf,
    d_in, d_own, d_send, d_parts, d_fin,
    ss, rs, lsem, wsem,
):
    f32, bf16 = jnp.float32, jnp.bfloat16
    r, f = lax.axis_index("rep"), lax.axis_index("fsdp")
    x, zh, c = r // 4, (r // 2) % 2, r % 2
    zl, y = f // 4, f % 4
    z = zh * 2 + zl

    def dev(dx=0, dy=0, dz=0, dc=0):
        z2 = (z + dz) % 4
        return dict(
            rep=((x + dx) % 4) * 4 + (z2 // 2) * 2 + (c + dc) % 2,
            fsdp=(z2 % 2) * 4 + (y + dy) % 4,
        )

    def zlow(zrel, dy):
        return dict(rep=r, fsdp=((zl + zrel) % 2) * 4 + (y + dy) % 4)

    def chip(dx, dzh):
        return dict(rep=((x + dx) % 4) * 4 + ((zh + dzh) % 2) * 2 + c, fsdp=f)

    core = dev(dc=1)

    def copy(ch, src, dst, device):
        return pltpu.make_async_remote_copy(
            src_ref=src, dst_ref=dst, send_sem=ss.at[ch], recv_sem=rs.at[ch], device_id=device
        )

    sent = []

    def send(ch, src, dst, device):
        cp = copy(ch, src, dst, device)
        cp.start()
        sent.append(cp)

    def got(ch, dst):
        copy(ch, dst, dst, core).wait_recv()

    own = pltpu.make_async_copy(kw.at[x, zh, c], wr.at[0, 0, c, 0], lsem.at[0])
    ltok = pltpu.make_async_copy(tok_hbm, tok, lsem.at[1])
    lcot = pltpu.make_async_copy(cot_hbm, cot.at[0, 0], lsem.at[2])
    ldel = pltpu.make_async_copy(deltas.at[c], d_own, lsem.at[3])
    for cp in (own, ltok, lcot, ldel):
        cp.start()

    barrier = pltpu.get_barrier_semaphore()
    partners = (
        [dev(dy=k) for k in (1, 2, 3)] + [dev(dz=k) for k in (1, 2, 3)] + [core]
        + [zlow(1, k) for k in (1, 2, 3)]
        + [chip(k, h) for k in (1, 2, 3) for h in (0, 1)]
    )
    for p in partners:
        pl.semaphore_signal(barrier, 1, device_id=p)
    pl.semaphore_wait(barrier, len(partners))

    send(E0, deltas.at[1 - c], d_in, core)
    for k in (1, 3, 2):
        send(A0 + k, kw.at[x, zh, c], wr.at[0, 0, c, 4 - k], dev(dy=k))
    send(C0, cot_hbm, cot.at[1, 0], zlow(1, 0))

    ldel.wait()
    got(E0, d_in)

    @pl.loop(0, HALF // 32)
    def _(i):
        rows = pl.ds(pl.multiple_of(i * 32, 32), 32)
        total = d_own[rows, :].astype(f32) + d_in[rows, :].astype(f32)
        total = total.astype(bf16)
        for q in range(8):
            d_send[q, rows, :] = total[:, q * 128:(q + 1) * 128]

    for q in (2, 6, 4, 1, 3, 5, 7):
        dx, dzh = q // 2, q % 2
        q2 = ((x + dx) % 4) * 2 + (zh + dzh) % 2
        back = ((4 - dx) % 4) * 2 + dzh
        send(E0 + q, d_send.at[q2], d_parts.at[back], chip(dx, dzh))

    ltok.wait()
    gainf[...] = gain_ref[...].astype(f32)
    rowacc[...] = jnp.zeros_like(rowacc)

    def cols_of(i):
        return pl.ds(pl.multiple_of(i * CH, 128), CH)

    def fold(v):
        return v[:, :128] + v[:, 128:256] + v[:, 256:384]

    @pl.loop(0, D // CH)
    def _(i):
        t = tok[:, cols_of(i)].astype(f32)
        rowacc[...] += fold(t * t)

    inv[...] = lax.rsqrt(jnp.sum(rowacc[...], axis=1, keepdims=True) / D + EPS)

    @pl.loop(0, D // CH)
    def _(i):
        t = tok[:, cols_of(i)].astype(f32)
        normed[:, cols_of(i)] = (t * inv[...] * gainf[:, cols_of(i)]).astype(bf16)

    rowacc[...] = jnp.zeros_like(rowacc)
    kacc[...] = jnp.zeros_like(kacc)

    own.wait()
    for k in (1, 3, 2):
        got(A0 + k, wr.at[0, 0, c, 4 - k])

    def part(xrel, g, lo, hi):
        return wr.at[xrel, g, c, pl.ds(lo, hi - lo)]

    def to_x(g):
        lo, hi = SPAN[g]
        send(X0 + g, part(0, g, lo, hi), part(3, g, lo, hi), dev(dx=1))
        send(X0 + 4 + g, part(0, g, lo, hi), part(1, g, lo, hi), dev(dx=3))
        send(D0 + g, part(0, g, lo, hi), part(0, g, lo, hi), core)

    def forward(g):
        lo, hi = SPAN[g]
        got(X0 + g, part(3, g, lo, hi))
        lo2, hi2 = FWD_P[g]
        send(F0 + g, part(3, g, lo2, hi2), part(2, g, lo2, hi2), dev(dx=1))
        send(D0 + 4 + g, part(3, g, lo, hi), part(3, g, lo, hi), core)
        got(X0 + 4 + g, part(1, g, lo, hi))
        lo2, hi2 = FWD_M[g]
        send(F0 + 4 + g, part(1, g, lo2, hi2), part(2, g, lo2, hi2), dev(dx=3))
        send(D0 + 8 + g, part(1, g, lo, hi), part(1, g, lo, hi), core)

    def swap(g):
        for at, (lo, hi) in ((0, FWD_P[g]), (4, FWD_M[g])):
            got(F0 + at + g, part(2, g, lo, hi))
            send(D0 + 12 + at + g, part(2, g, lo, hi), part(2, g, lo, hi), core)

    for k in (1, 3, 2):
        lo, hi = SPAN[k]
        send(B0 + k, part(0, 0, lo, hi), part(0, 4 - k, lo, hi), dev(dz=k))
    to_x(0)

    def block(s):
        f2 = ((zl + s // 4) % 2) * 4 + (y + s % 4) % 4
        back = (s // 4) * 4 + (4 - s % 4) % 4
        cols = pl.ds(pl.multiple_of(f2 * SHARD, 128), SHARD)
        send(T0 + s, normed.at[:, cols], slab.at[back], zlow(s // 4, s % 4))

    for s in (1, 3, 2):
        block(s)

    lcot.wait()
    got(C0, cot.at[1, 0])
    for k in (1, 3, 2):
        send(C0 + k, cot.at[:, 0], cot.at[:, 4 - k], dev(dy=k))

    def chunk(slot, col):
        cols = pl.ds(pl.multiple_of(col, 128), CH)
        w = wbuf[slot].reshape(CH, KW)
        kacc[...] += jnp.dot(normed[:, cols], w, preferred_element_type=f32)
        up = lax.dot_general(
            cot[0, 0], w, (((1,), (1,)), ((), ())), preferred_element_type=f32
        )
        up = up * gainf[:, cols]
        rowacc[...] += fold(up * tok[:, cols].astype(f32))
        u[:, cols] = up * inv[...]

    def run(n, first, fetch, column):
        for cp in fetch(first, 0):
            cp.start()

        @pl.loop(0, n)
        def _(i):
            slot = i % 2

            @pl.when(i < n - 1)
            def _():
                for cp in fetch(first + i + 1, 1 - slot):
                    cp.start()

            for cp in fetch(first + i, slot):
                cp.wait()
            chunk(slot, column(first + i))

    def fetch_own(i, slot):
        return [pltpu.make_async_copy(kw.at[i, h], wbuf.at[slot, h], wsem.at[slot, h]) for h in (0, 1)]

    run(4, 0, fetch_own, lambda i: f * SHARD + i * CH)

    def chunks(xrel, first, n):
        def fetch(i, slot):
            low = (zl + i // 4) % 2
            return [
                pltpu.make_async_copy(
                    wr.at[xrel, (h * 2 + low - z + 4) % 4, :, i % 4],
                    wbuf.at[slot, h], wsem.at[slot, h],
                )
                for h in (0, 1)
            ]

        def column(i):
            f2 = ((zl + i // 4) % 2) * 4 + (y + i % 4) % 4
            return f2 * SHARD + ((x + xrel) % 4) * CH

        run(n, first, fetch, column)

    def got_core(base, xrel, g, lo, hi):
        got(base + g, wr.at[xrel, g, 1 - c, pl.ds(lo, hi - lo)])

    for g in (1, 3):
        got(B0 + 4 - g, part(0, g, *SPAN[g]))
        to_x(g)
    forward(0)
    got(B0 + 2, part(0, 2, *SPAN[2]))
    to_x(2)
    for s in (4, 5, 7, 6):
        block(s)

    for g in range(4):
        got_core(D0, 0, g, *SPAN[g])
    chunks(0, 1, 7)
    forward(1)

    def weight(src, col0, place, first=False):
        @pl.loop(0, SHARD // CH)
        def _(i):
            lhs = src[:, pl.ds(pl.multiple_of(col0 + i * CH, 128), CH)]
            rows = pl.ds(pl.multiple_of(i * CH, CH), CH)
            new = lax.dot_general(
                lhs, place[...], (((0,), (0,)), ((), ())), preferred_element_type=f32
            )
            if first:
                acc[rows, :] = new
            else:
                acc[rows, :] += new

    weight(normed, f * SHARD, cot.at[0, 0], True)
    forward(3)
    swap(0)

    for q in range(1, 8):
        dx, dzh = q // 2, q % 2
        got(E0 + q, d_parts.at[((4 - dx) % 4) * 2 + dzh])

    @pl.loop(0, HALF // 64)
    def _(i):
        rows = pl.ds(pl.multiple_of(i * 64, 64), 64)
        total = d_send[x * 2 + zh, rows, :].astype(f32)
        for q in range(1, 8):
            total = total + d_parts[q, rows, :].astype(f32)
        d_fin[c, rows, :] = total

    send(G0, d_fin.at[c], d_fin.at[c], core)
    forward(2)

    for g in range(4):
        got_core(D0 + 4, 3, g, *SPAN[g])
        got_core(D0 + 8, 1, g, *SPAN[g])
    chunks(3, 1, 7)
    swap(1)
    chunks(1, 1, 7)
    for k in (1, 3, 2):
        got(C0 + k, cot.at[:, 4 - k])
    for s in (1, 3, 2):
        back = (4 - s) % 4
        got(T0 + s, slab.at[back])
        weight(slab.at[back], 0, cot.at[0, back])
    swap(3)
    got(G0, d_fin.at[1 - c])
    dsum_ref[...] = d_fin[...]
    swap(2)

    for g in range(4):
        got_core(D0 + 12, 2, g, *FWD_P[g])
        got_core(D0 + 16, 2, g, *FWD_M[g])
    chunks(2, 1, 7)
    keys_ref[...] = kacc[...].astype(bf16)

    inner = jnp.sum(rowacc[...], axis=1, keepdims=True) / D
    i1 = inv[...]
    scale = i1 * i1 * i1 * inner
    inv[...] = scale

    def out(i):
        cols = pl.ds(pl.multiple_of(i * SHARD, 128), SHARD)
        return pltpu.make_async_copy(tok.at[:, cols], tg_hbm.at[:, cols], lsem.at[i])

    for i in range(8):
        @pl.loop(0, SHARD // CH)
        def _(j):
            cols = pl.ds(pl.multiple_of(i * SHARD + j * CH, 128), CH)
            t = tok[:, cols].astype(f32)
            tok[:, cols] = (u[:, cols] - t * inv[...]).astype(bf16)
        out(i).start()

    for s in (4, 5, 7, 6):
        back = 4 + (4 - s % 4) % 4
        got(T0 + s, slab.at[back])
        weight(slab.at[back], 0, cot.at[1, back - 4])

    @pl.loop(0, SHARD // CH)
    def _(i):
        rows = pl.ds(pl.multiple_of(i * CH, CH), CH)
        wg_ref[rows, :] = acc[rows, :].astype(bf16)

    for i in range(8):
        out(i).wait()
    for cp in sent:
        cp.wait_send()


def on_device(tokens, norm_gain, key_weight, cotangent, outer_deltas, anchor, momentum):
    f32, bf16 = jnp.float32, jnp.bfloat16
    any_space, vmem = pl.BlockSpec(memory_space=pl.ANY), pl.BlockSpec(memory_space=pltpu.VMEM)
    keys, token_grad, weight_grad, delta_sum, _ = pl.pallas_call(
        kernel,
        out_shape=(
            jax.ShapeDtypeStruct((TOK, KW), bf16),
            jax.ShapeDtypeStruct((TOK, D), bf16),
            jax.ShapeDtypeStruct((SHARD, KW), bf16),
            jax.ShapeDtypeStruct((2, HALF, 128), f32),
            jax.ShapeDtypeStruct((4, 4, 2, 4, PIECE, KW), bf16),
        ),
        in_specs=[any_space, vmem, any_space, any_space, any_space],
        out_specs=(vmem, any_space, vmem, vmem, any_space),
        scratch_shapes=[
            pltpu.VMEM((TOK, D), bf16),
            pltpu.VMEM((TOK, D), bf16),
            pltpu.VMEM((TOK, D), f32),
            pltpu.VMEM((8, TOK, SHARD), bf16),
            pltpu.VMEM((2, 4, TOK, KW), bf16),
            pltpu.VMEM((SHARD, KW), f32),
            pltpu.VMEM((TOK, KW), f32),
            pltpu.VMEM((1, D), f32),
            pltpu.VMEM((TOK, 1), f32),
            pltpu.VMEM((TOK, 128), f32),
            pltpu.VMEM((2, 2, 2, PIECE, KW), bf16),
            pltpu.VMEM((HALF, KW), bf16),
            pltpu.VMEM((HALF, KW), bf16),
            pltpu.VMEM((8, HALF, 128), bf16),
            pltpu.VMEM((8, HALF, 128), bf16),
            pltpu.VMEM((2, HALF, 128), f32),
            pltpu.SemaphoreType.DMA((NCH,)),
            pltpu.SemaphoreType.DMA((NCH,)),
            pltpu.SemaphoreType.DMA((8,)),
            pltpu.SemaphoreType.DMA((2, 2)),
        ],
        compiler_params=pltpu.CompilerParams(
            collective_id=0, has_side_effects=True, vmem_limit_bytes=62 * 1024 * 1024
        ),
        cost_estimate=pl.CostEstimate(
            flops=6 * TOK * D * KW, bytes_accessed=100_000_000, transcendentals=0
        ),
        name="step",
    )(
        tokens,
        norm_gain.reshape(1, D),
        key_weight.reshape(4, 2, 2, PIECE, KW),
        cotangent,
        outer_deltas.reshape(2, HALF, KW),
    )
    delta_sum = delta_sum.reshape(SHARD, 128)
    odd = lax.axis_index("rep") % 2 == 1
    mean_delta = jnp.where(odd, delta_sum[:, 64:], delta_sum[:, :64]) / lax.axis_size("rep")
    new_momentum = OUTER_MU * momentum + mean_delta
    new_anchor = anchor - OUTER_LR * (mean_delta + OUTER_MU * new_momentum)
    return (keys, token_grad, weight_grad[None], new_anchor, new_momentum)


def solution(mesh):
    return jax.shard_map(
        on_device,
        mesh=mesh,
        in_specs=(
            P(("rep", "fsdp"), None),
            P(),
            P("fsdp", None),
            P(("rep", "fsdp"), None),
            P("rep", "fsdp", None),
            P("fsdp", "rep"),
            P("fsdp", "rep"),
        ),
        out_specs=(
            P(("rep", "fsdp"), None),
            P(("rep", "fsdp"), None),
            P("rep", "fsdp", None),
            P("fsdp", "rep"),
            P("fsdp", "rep"),
        ),
        check_vma=False,
    )
```

time: 661 us -> 175 us (0.26)
  waiting for transfers between devices: 580 us -> 0 us
  Pallas kernels: 0 us -> 159 us
  matrix products: 48 us -> 0 us
  between operations: 15.5 us -> 0.7 us
  other arithmetic: 11.8 us -> 1 us
  local copies, waits for them, and re-layouts: 4.67 us -> 12.3 us
    psum x1 -> x0, waiting for transfers between devices: 328 us -> none  [on_device(): lax.psum(delta_terms.astype(jnp.bfloat16), 'rep').astype(jnp.float32)]
    all_gather x1 -> x0, waiting for transfers between devices: 252 us -> none  [on_device(): shard_rows = lax.all_gather(key_weight, 'fsdp', axis=0, tiled=True)]
    pallas_call x0 -> x1, Pallas kernels: none -> 159 us  [on_device(): pl.pallas_call(kernel, out_shape=(jax.ShapeDtypeStruct((TOK, KW), bf16),...]
    dot_general x3 -> x0, matrix products: 48 us -> none  [the longest x1 18.4 us: on_device(): lax.dot_general(cotangent, shard_rows, (((1,), (1,)), ((), ())), preferre...]
    convert_element_type x2 -> x0, other arithmetic: 9.84 us -> none  [the longest x1 9.83 us: on_device(): (inv_rms * upstream - tok_f * inv_rms ** 3 * inner_mean).astype(jnp.bfloa...]
  transfers between devices with their start and end apart: 3 -> 0, of which waited for: 2 -> 0; matrix products, arithmetic and copies ran while one was open for 10% -> 0% of each run, Pallas kernels for 0% -> 0%
where the time goes in v1:
time: 175 us; the launch traced here: 173 us
  Pallas kernels  159 us (91%)
  local copies, waits for them, and re-layouts  12.3 us (7%)
    pallas_call x1, Pallas kernels, on_device(): pl.pallas_call(kernel, out_shape=(jax.ShapeDtypeStruct((TOK, KW), bf16),...  159 us
    unnamed x13, local copies, waits for them, and re-layouts  9.26 us

profile of v1, /device:TPU:1, one launch (start us, length us, event | category | flops | bytes accessed | tf_op | source)
XLA Modules:
  0.0 173.4 jit_solution(8996098822373538688)
XLA Ops:
  0.6 1.4 reshape.22.gain_ref
  2.0 0.0 copy-start.2
  2.0 0.0 copy-start.3
  2.0 159.3 %step.1 = (bf16[256,1024]{1,0:T(8,128)(2,1)}, bf16[256,12288]{1,0:T(8,128)(2,1)}, bf16[1536,1024]{1,0:T(8,128)(2,1)}, f32[2,768,128]{2,1,0:T(8,128)}, bf16[4,4,2,4,96,1024]{5,4,3,2,1,0:T(8,128)(2,1)}) custom-call(bf16[256,12288]{1,0:T(8,128)(2,1)} %tok_hbm.1, bf16[1,12288]{1,0:T(2,128)(2,1)} %reshape.22.gain_ref, bf16[4,2,2,96,1024]{4,3,2,1,0:T(8,128)(2,1)} %bitcast.6, ...), custom_call_target="tpu_custom_call" | custom-call | flops 19327352832 | bytes 100000000 | tf_op jit(solution)/shard_map/step/pallas_call | solution.py:351
  161.4 0.0 copy-start.1
  161.4 1.7 fusion
  163.1 0.2 copy.14
  163.3 0.2 copy.15
  163.6 0.0 copy-done.2
  163.6 0.0 copy-done.3
  163.6 1.0 multiply_subtract_fusion
  164.6 0.0 copy-done.1
  164.6 0.8 copy.19
  165.4 0.0 copy-start
  165.4 6.3 %copy.20 = bf16[256,12288]{1,0:T(8,128)(2,1)} copy(bf16[256,12288]{1,0:T(8,128)(2,1)} %get-tuple-element.23) | data formatting | bytes 12582912
  171.7 0.0 copy-done
  171.7 1.7 copy.21
Async XLA Ops:
  2.0 161.6 %copy-start.2 = (f32[1536,64]{0,1:T(8,128)S(1)}, f32[1536,64]{0,1:T(8,128)}, u32[]{:S(2)}) copy-start(f32[1536,64]{0,1:T(8,128)} %param.12) | copy-start | bytes 1179652
  2.0 161.6 %copy-start.3 = (f32[1536,64]{0,1:T(8,128)S(1)}, f32[1536,64]{0,1:T(8,128)}, u32[]{:S(2)}) copy-start(f32[1536,64]{0,1:T(8,128)} %param.13) | copy-start | bytes 1179652
  161.4 3.3 %copy-start.1 = (bf16[256,1024]{1,0:T(8,128)(2,1)S(1)}, bf16[256,1024]{1,0:T(8,128)(2,1)}, u32[]{:S(2)}) copy-start(bf16[256,1024]{1,0:T(8,128)(2,1)} %get-tuple-element.22) | copy-start | bytes 1572868
  165.4 6.3 %copy-start = (bf16[1536,1024]{1,0:T(8,128)(2,1)S(1)}, bf16[1536,1024]{1,0:T(8,128)(2,1)}, u32[]{:S(2)}) copy-start(bf16[1536,1024]{1,0:T(8,128)(2,1)} %get-tuple-element.11) | copy-start | bytes 9437188

commit v2 on v1

v2 whole, which is shorter than its diff:
```python
import functools

import jax
import jax.numpy as jnp
from jax import lax
from jax.experimental import pallas as pl
from jax.experimental.pallas import tpu as pltpu
from jax.sharding import PartitionSpec as P

EPS = 1e-05
OUTER_LR = 0.7
OUTER_MU = 0.9

TOK = 256
D = 12288
KW = 1024
SHARD = 1536
PIECE = 96
CH = 384
HALF = 768

A0 = 0
B0 = 4
X0 = 8
F0 = 16
D0 = 24
C0 = 44
E0 = 48
G0 = 52
R0 = 54
T0 = 58
NCH = 90

SPAN = ((1, 4), (0, 4), (1, 4), (0, 4))
FWD_P = ((1, 3), (0, 2), (1, 2), (0, 2))
FWD_M = ((3, 4), (2, 4), (2, 4), (2, 4))


def kernel(
    tok_hbm, gain_ref, kw, cot_hbm, deltas,
    keys_ref, tg_hbm, wg_ref, dsum_ref, wr,
    tok, normed, u, slab, cot, rs_out, rs_in, kacc, gainf, inv, rowacc, wbuf,
    d_in, d_own, d_send, d_parts, d_half, d_far, d_fin,
    ss, rs, lsem, wsem,
):
    f32, bf16 = jnp.float32, jnp.bfloat16
    r, f = lax.axis_index("rep"), lax.axis_index("fsdp")
    x, zh, c = r // 4, (r // 2) % 2, r % 2
    zl, y = f // 4, f % 4
    z = zh * 2 + zl

    def dev(dx=0, dy=0, dz=0, dc=0):
        z2 = (z + dz) % 4
        return dict(
            rep=((x + dx) % 4) * 4 + (z2 // 2) * 2 + (c + dc) % 2,
            fsdp=(z2 % 2) * 4 + (y + dy) % 4,
        )

    core = dev(dc=1)
    beside = dict(rep=r, fsdp=(1 - zl) * 4 + y)

    def copy(ch, src, dst, device):
        return pltpu.make_async_remote_copy(
            src_ref=src, dst_ref=dst, send_sem=ss.at[ch], recv_sem=rs.at[ch], device_id=device
        )

    sent = []

    def send(ch, src, dst, device):
        cp = copy(ch, src, dst, device)
        cp.start()
        sent.append(cp)

    def got(ch, dst):
        copy(ch, dst, dst, core).wait_recv()

    own = pltpu.make_async_copy(kw.at[x, zh, c], wr.at[0, 0, c, 0], lsem.at[0])
    ldel = pltpu.make_async_copy(deltas.at[c], d_own, lsem.at[3])
    ltok = pltpu.make_async_copy(tok_hbm, tok, lsem.at[1])
    lcot = pltpu.make_async_copy(cot_hbm, cot.at[0], lsem.at[2])
    for cp in (ldel, own, ltok, lcot):
        cp.start()

    barrier = pltpu.get_barrier_semaphore()
    partners = (
        [dev(dy=k) for k in (1, 2, 3)] + [dev(dz=k) for k in (1, 2, 3)]
        + [dev(dx=k) for k in (1, 2, 3)] + [core]
    )
    for p in partners:
        pl.semaphore_signal(barrier, 1, device_id=p)
    pl.semaphore_wait(barrier, len(partners))

    send(E0, deltas.at[1 - c], d_in, core)
    for k in (1, 3, 2):
        send(A0 + k, kw.at[x, zh, c], wr.at[0, 0, c, 4 - k], dev(dy=k))
    for k in (1, 3, 2):
        send(C0 + k, cot_hbm, cot.at[4 - k], dev(dy=k))

    ldel.wait()
    got(E0, d_in)

    @pl.loop(0, HALF // 32)
    def _(i):
        rows = pl.ds(pl.multiple_of(i * 32, 32), 32)
        for q in range(8):
            cols = slice(q * 128, (q + 1) * 128)
            total = d_own[rows, cols].astype(f32) + d_in[rows, cols].astype(f32)
            d_send[q, rows, :] = total.astype(bf16)

    for k in (1, 3, 2):
        send(E0 + k, d_send.at[pl.ds(((x + k) % 4) * 2, 2)], d_parts.at[4 - k], dev(dx=k))

    own.wait()
    for k in (1, 3, 2):
        got(A0 + k, wr.at[0, 0, c, 4 - k])

    def part(xrel, g, lo, hi):
        return wr.at[xrel, g, c, pl.ds(lo, hi - lo)]

    def to_x(g):
        lo, hi = SPAN[g]
        send(X0 + g, part(0, g, lo, hi), part(3, g, lo, hi), dev(dx=1))
        send(X0 + 4 + g, part(0, g, lo, hi), part(1, g, lo, hi), dev(dx=3))
        send(D0 + g, part(0, g, lo, hi), part(0, g, lo, hi), core)

    def forward(g):
        lo, hi = SPAN[g]
        got(X0 + g, part(3, g, lo, hi))
        lo2, hi2 = FWD_P[g]
        send(F0 + g, part(3, g, lo2, hi2), part(2, g, lo2, hi2), dev(dx=1))
        send(D0 + 4 + g, part(3, g, lo, hi), part(3, g, lo, hi), core)
        got(X0 + 4 + g, part(1, g, lo, hi))
        lo2, hi2 = FWD_M[g]
        send(F0 + 4 + g, part(1, g, lo2, hi2), part(2, g, lo2, hi2), dev(dx=3))
        send(D0 + 8 + g, part(1, g, lo, hi), part(1, g, lo, hi), core)

    def swap(g):
        for at, (lo, hi) in ((0, FWD_P[g]), (4, FWD_M[g])):
            got(F0 + at + g, part(2, g, lo, hi))
            send(D0 + 12 + at + g, part(2, g, lo, hi), part(2, g, lo, hi), core)

    for k in (1, 3, 2):
        lo, hi = SPAN[k]
        send(B0 + k, part(0, 0, lo, hi), part(0, 4 - k, lo, hi), dev(dz=k))
    to_x(0)

    def cols_of(i):
        return pl.ds(pl.multiple_of(i * CH, 128), CH)

    def fold(v):
        return v[:, :128] + v[:, 128:256] + v[:, 256:384]

    def wide(v):
        return jnp.concatenate([v, v, v], axis=1)

    ltok.wait()
    gainf[...] = gain_ref[...].astype(f32)
    rowacc[...] = jnp.zeros_like(rowacc)

    @pl.loop(0, D // CH)
    def _(i):
        t = tok[:, cols_of(i)].astype(f32)
        rowacc[...] += fold(t * t)

    mean = jnp.sum(rowacc[...], axis=1, keepdims=True) / D
    inv[...] = jnp.broadcast_to(lax.rsqrt(mean + EPS), inv.shape)

    @pl.loop(0, D // CH)
    def _(i):
        t = tok[:, cols_of(i)].astype(f32)
        normed[:, cols_of(i)] = (t * wide(inv[...]) * gainf[:, cols_of(i)]).astype(bf16)

    rowacc[...] = jnp.zeros_like(rowacc)
    kacc[...] = jnp.zeros_like(kacc)

    def feature(j, dy):
        low = (zl + 1 - j // 4) % 2
        return pl.ds(pl.multiple_of((low * 4 + (y + dy) % 4) * SHARD + (j % 4) * CH, 128), CH)

    def block(j):
        for k in (1, 3, 2):
            send(T0 + 4 * j + k, normed.at[:, feature(j, k)], slab.at[j, 4 - k], dev(dy=k))

    def product(j):
        for k in (1, 3, 2):
            got(T0 + 4 * j + k, slab.at[j, 4 - k])
        slab[j, 0] = normed[:, feature(j, 0)]
        return lax.dot_general(
            slab[j].reshape(4 * TOK, CH), cot[...].reshape(4 * TOK, KW),
            (((0,), (0,)), ((), ())), preferred_element_type=f32,
        )

    def reduce(j):
        rs_out[j] = product(j).astype(bf16)
        send(R0 + j, rs_out.at[j], rs_in.at[j], beside)

    def weight(j):
        total = product(4 + j)
        got(R0 + j, rs_in.at[j])
        wg_ref[pl.ds(j * CH, CH), :] = (total + rs_in[j].astype(f32)).astype(bf16)

    block(0)
    block(1)
    lcot.wait()

    def chunk(slot, col):
        cols = pl.ds(pl.multiple_of(col, 128), CH)
        w = wbuf[slot].reshape(CH, KW)
        kacc[...] += jnp.dot(normed[:, cols], w, preferred_element_type=f32)
        up = lax.dot_general(
            cot[0], w, (((1,), (1,)), ((), ())), preferred_element_type=f32
        )
        up = up * gainf[:, cols]
        rowacc[...] += fold(up * tok[:, cols].astype(f32))
        u[:, cols] = up * wide(inv[...])

    def run(n, first, fetch, column):
        for cp in fetch(first, 0):
            cp.start()

        @pl.loop(0, n)
        def _(i):
            slot = i % 2

            @pl.when(i < n - 1)
            def _():
                for cp in fetch(first + i + 1, 1 - slot):
                    cp.start()

            for cp in fetch(first + i, slot):
                cp.wait()
            chunk(slot, column(first + i))

    def own_chunks():
        def fetch(i, slot):
            return [pltpu.make_async_copy(kw.at[i, h], wbuf.at[slot, h], wsem.at[slot, h]) for h in (0, 1)]

        run(4, 0, fetch, lambda i: f * SHARD + i * CH)

    def chunks(xrel, first, n):
        def fetch(i, slot):
            low = (zl + i // 4) % 2
            return [
                pltpu.make_async_copy(
                    wr.at[xrel, (h * 2 + low - z + 4) % 4, :, i % 4],
                    wbuf.at[slot, h], wsem.at[slot, h],
                )
                for h in (0, 1)
            ]

        def column(i):
            f2 = ((zl + i // 4) % 2) * 4 + (y + i % 4) % 4
            return f2 * SHARD + ((x + xrel) % 4) * CH

        run(n, first, fetch, column)

    def got_core(base, xrel, g, lo, hi):
        got(base + g, wr.at[xrel, g, 1 - c, pl.ds(lo, hi - lo)])

    own_chunks()
    for g in (1, 3):
        got(B0 + 4 - g, part(0, g, *SPAN[g]))
        to_x(g)
    forward(0)

    for k in (1, 3, 2):
        got(E0 + k, d_parts.at[4 - k])

    def over_x(half, rows):
        total = d_send[x * 2 + half, rows, :].astype(f32)
        for k in (1, 2, 3):
            total = total + d_parts[k, half, rows, :].astype(f32)
        return total

    @pl.loop(0, HALF // 64)
    def _(i):
        rows = pl.ds(pl.multiple_of(i * 64, 64), 64)
        d_half[rows, :] = over_x(1 - zh, rows).astype(bf16)

    send(G0, d_half, d_far, dev(dz=2))

    for k in (1, 3, 2):
        got(C0 + k, cot.at[4 - k])
    reduce(0)
    block(2)
    got(B0 + 2, part(0, 2, *SPAN[2]))
    to_x(2)
    reduce(1)
    block(3)
    for g in range(4):
        got_core(D0, 0, g, *SPAN[g])
    forward(1)
    chunks(0, 1, 3)
    reduce(2)
    block(4)
    chunks(0, 4, 4)
    forward(3)
    reduce(3)
    block(5)
    swap(0)

    got(G0, d_far)

    @pl.loop(0, HALF // 64)
    def _(i):
        rows = pl.ds(pl.multiple_of(i * 64, 64), 64)
        d_fin[c, rows, :] = over_x(zh, rows) + d_far[rows, :].astype(f32)

    send(G0 + 1, d_fin.at[c], d_fin.at[c], core)

    weight(0)
    block(6)
    forward(2)
    for g in (1, 3):
        got_core(D0 + 4, 3, g, *SPAN[g])
        got_core(D0 + 8, 1, g, *SPAN[g])
    chunks(3, 4, 4)
    chunks(1, 4, 4)
    weight(1)
    block(7)
    swap(1)
    for g in (0, 2):
        got_core(D0 + 4, 3, g, *SPAN[g])
        got_core(D0 + 8, 1, g, *SPAN[g])
    chunks(3, 1, 3)
    chunks(1, 1, 3)
    weight(2)
    swap(3)
    got(G0 + 1, d_fin.at[1 - c])
    dsum_ref[...] = d_fin[...]
    for g in (1, 3):
        got_core(D0 + 12, 2, g, *FWD_P[g])
        got_core(D0 + 16, 2, g, *FWD_M[g])
    chunks(2, 4, 4)
    swap(2)
    for g in (0, 2):
        got_core(D0 + 12, 2, g, *FWD_P[g])
        got_core(D0 + 16, 2, g, *FWD_M[g])
    chunks(2, 1, 3)
    keys_ref[...] = kacc[...].astype(bf16)

    i1 = inv[...]
    inner = jnp.sum(rowacc[...], axis=1, keepdims=True) / D
    inv[...] = i1 * i1 * i1 * inner

    def out(i):
        cols = pl.ds(pl.multiple_of(i * SHARD, 128), SHARD)
        return pltpu.make_async_copy(tok.at[:, cols], tg_hbm.at[:, cols], lsem.at[i])

    for i in range(8):
        @pl.loop(0, SHARD // CH)
        def _(j):
            cols = pl.ds(pl.multiple_of(i * SHARD + j * CH, 128), CH)
            t = tok[:, cols].astype(f32)
            tok[:, cols] = (u[:, cols] - t * wide(inv[...])).astype(bf16)
        out(i).start()

    weight(3)
    for i in range(8):
        out(i).wait()
    for cp in sent:
        cp.wait_send()


def on_device(tokens, norm_gain, key_weight, cotangent, outer_deltas, anchor, momentum):
    f32, bf16 = jnp.float32, jnp.bfloat16
    any_space, vmem = pl.BlockSpec(memory_space=pl.ANY), pl.BlockSpec(memory_space=pltpu.VMEM)
    keys, token_grad, weight_grad, delta_sum, _ = pl.pallas_call(
        kernel,
        out_shape=(
            jax.ShapeDtypeStruct((TOK, KW), bf16),
            jax.ShapeDtypeStruct((TOK, D), bf16),
            jax.ShapeDtypeStruct((SHARD, KW), bf16),
            jax.ShapeDtypeStruct((2, HALF, 128), f32),
            jax.ShapeDtypeStruct((4, 4, 2, 4, PIECE, KW), bf16),
        ),
        in_specs=[any_space, vmem, any_space, any_space, any_space],
        out_specs=(vmem, any_space, vmem, vmem, any_space),
        scratch_shapes=[
            pltpu.VMEM((TOK, D), bf16),
            pltpu.VMEM((TOK, D), bf16),
            pltpu.VMEM((TOK, D), f32),
            pltpu.VMEM((8, 4, TOK, CH), bf16),
            pltpu.VMEM((4, TOK, KW), bf16),
            pltpu.VMEM((4, CH, KW), bf16),
            pltpu.VMEM((4, CH, KW), bf16),
            pltpu.VMEM((TOK, KW), f32),
            pltpu.VMEM((1, D), f32),
            pltpu.VMEM((TOK, 128), f32),
            pltpu.VMEM((TOK, 128), f32),
            pltpu.VMEM((2, 2, 2, PIECE, KW), bf16),
            pltpu.VMEM((HALF, KW), bf16),
            pltpu.VMEM((HALF, KW), bf16),
            pltpu.VMEM((8, HALF, 128), bf16),
            pltpu.VMEM((4, 2, HALF, 128), bf16),
            pltpu.VMEM((HALF, 128), bf16),
            pltpu.VMEM((HALF, 128), bf16),
            pltpu.VMEM((2, HALF, 128), f32),
            pltpu.SemaphoreType.DMA((NCH,)),
            pltpu.SemaphoreType.DMA((NCH,)),
            pltpu.SemaphoreType.DMA((8,)),
            pltpu.SemaphoreType.DMA((2, 2)),
        ],
        compiler_params=pltpu.CompilerParams(
            collective_id=0, has_side_effects=True, vmem_limit_bytes=62 * 1024 * 1024
        ),
        cost_estimate=pl.CostEstimate(
            flops=6 * TOK * D * KW, bytes_accessed=100_000_000, transcendentals=0
        ),
        name="step",
    )(
        tokens,
        norm_gain.reshape(1, D),
        key_weight.reshape(4, 2, 2, PIECE, KW),
        cotangent,
        outer_deltas.reshape(2, HALF, KW),
    )
    delta_sum = delta_sum.reshape(SHARD, 128)
    odd = lax.axis_index("rep") % 2 == 1
    mean_delta = jnp.where(odd, delta_sum[:, 64:], delta_sum[:, :64]) / lax.axis_size("rep")
    new_momentum = OUTER_MU * momentum + mean_delta
    new_anchor = anchor - OUTER_LR * (mean_delta + OUTER_MU * new_momentum)
    return (keys, token_grad, weight_grad[None], new_anchor, new_momentum)


def solution(mesh):
    return jax.shard_map(
        on_device,
        mesh=mesh,
        in_specs=(
            P(("rep", "fsdp"), None),
            P(),
            P("fsdp", None),
            P(("rep", "fsdp"), None),
            P("rep", "fsdp", None),
            P("fsdp", "rep"),
            P("fsdp", "rep"),
        ),
        out_specs=(
            P(("rep", "fsdp"), None),
            P(("rep", "fsdp"), None),
            P("rep", "fsdp", None),
            P("fsdp", "rep"),
            P("fsdp", "rep"),
        ),
        check_vma=False,
    )
```

time: 175 us -> 150 us (0.86)
  Pallas kernels: 159 us -> 135 us
    pallas_call x1, Pallas kernels: 159 us -> 135 us  [on_device(): pl.pallas_call(kernel, out_shape=(jax.ShapeDtypeStruct((TOK, KW), bf16),...]
where the time goes in v2:
time: 150 us; the launch traced here: 149 us
  Pallas kernels  135 us (90%)
  local copies, waits for them, and re-layouts  12.3 us (8%)
    pallas_call x1, Pallas kernels, on_device(): pl.pallas_call(kernel, out_shape=(jax.ShapeDtypeStruct((TOK, KW), bf16),...  135 us
    unnamed x13, local copies, waits for them, and re-layouts  9.26 us

profile of v2, /device:TPU:1, one launch (start us, length us, event | category | flops | bytes accessed | tf_op | source)
XLA Modules:
  0.0 148.9 jit_solution(7670804907492116397)
XLA Ops:
  0.6 1.4 reshape.22.gain_ref
  2.0 0.0 copy-start.2
  2.0 0.0 copy-start.3
  2.0 134.9 %step.1 = (bf16[256,1024]{1,0:T(8,128)(2,1)}, bf16[256,12288]{1,0:T(8,128)(2,1)}, bf16[1536,1024]{1,0:T(8,128)(2,1)}, f32[2,768,128]{2,1,0:T(8,128)}, bf16[4,4,2,4,96,1024]{5,4,3,2,1,0:T(8,128)(2,1)}) custom-call(bf16[256,12288]{1,0:T(8,128)(2,1)} %tok_hbm.1, bf16[1,12288]{1,0:T(2,128)(2,1)} %reshape.22.gain_ref, bf16[4,2,2,96,1024]{4,3,2,1,0:T(8,128)(2,1)} %bitcast.6, ...), custom_call_target="tpu_custom_call" | custom-call | flops 19327352832 | bytes 100000000 | tf_op jit(solution)/shard_map/step/pallas_call | solution.py:368
  136.9 0.0 copy-start.1
  136.9 1.7 %fusion = (f32[1536,64]{1,0:T(8,128)S(1)}, f32[1536,64]{1,0:T(8,128)S(1)}) fusion(f32[1536,128]{1,0:T(8,128)} %bitcast.5), kind=kLoop, calls=%fused_computation.3 | loop fusion | bytes 1572864 | tf_op jit(solution)/shard_map/slice | solution.py:420
  138.6 0.2 copy.14
  138.8 0.2 copy.15
  139.1 0.0 copy-done.2
  139.1 0.0 copy-done.3
  139.1 1.0 multiply_subtract_fusion
  140.1 0.0 copy-done.1
  140.1 0.8 copy.19
  140.9 0.0 copy-start
  140.9 6.3 %copy.20 = bf16[256,12288]{1,0:T(8,128)(2,1)} copy(bf16[256,12288]{1,0:T(8,128)(2,1)} %get-tuple-element.23) | data formatting | bytes 12582912
  147.2 0.0 copy-done
  147.2 1.7 %copy.21 = bf16[1,1536,1024]{2,1,0:T(8,128)(2,1)} copy(bf16[1,1536,1024]{2,1,0:T(8,128)(2,1)S(1)} %bitcast.4) | data formatting | bytes 6291456
Async XLA Ops:
  2.0 137.1 %copy-start.2 = (f32[1536,64]{0,1:T(8,128)S(1)}, f32[1536,64]{0,1:T(8,128)}, u32[]{:S(2)}) copy-start(f32[1536,64]{0,1:T(8,128)} %param.12) | copy-start | bytes 1179652
  2.0 137.1 %copy-start.3 = (f32[1536,64]{0,1:T(8,128)S(1)}, f32[1536,64]{0,1:T(8,128)}, u32[]{:S(2)}) copy-start(f32[1536,64]{0,1:T(8,128)} %param.13) | copy-start | bytes 1179652
  136.9 3.3 %copy-start.1 = (bf16[256,1024]{1,0:T(8,128)(2,1)S(1)}, bf16[256,1024]{1,0:T(8,128)(2,1)}, u32[]{:S(2)}) copy-start(bf16[256,1024]{1,0:T(8,128)(2,1)} %get-tuple-element.22) | copy-start | bytes 1572868
  140.9 6.3 %copy-start = (bf16[1536,1024]{1,0:T(8,128)(2,1)S(1)}, bf16[1536,1024]{1,0:T(8,128)(2,1)}, u32[]{:S(2)}) copy-start(bf16[1536,1024]{1,0:T(8,128)(2,1)} %get-tuple-element.11) | copy-start | bytes 9437188

commit v3 on v2

--- a/solution.py
+++ b/solution.py
@@ -23,25 +23,29 @@
 B0 = 4
 X0 = 8
 F0 = 16
+H0 = 20
 D0 = 24
 C0 = 44
 E0 = 48
 G0 = 52
 R0 = 54
 T0 = 58
-NCH = 90
+K0 = 90
+NCH = 91
+
+LIMIT = 57 * 1024 * 1024
+FINISH_LIMIT = 58 * 1024 * 1024
 
 SPAN = ((1, 4), (0, 4), (1, 4), (0, 4))
-FWD_P = ((1, 3), (0, 2), (1, 2), (0, 2))
-FWD_M = ((3, 4), (2, 4), (2, 4), (2, 4))
+FWD_P, FWD_M = (0, 2), (2, 4)
 
 
 def kernel(
     tok_hbm, gain_ref, kw, cot_hbm, deltas,
-    keys_ref, tg_hbm, wg_ref, dsum_ref, wr,
-    tok, normed, u, slab, cot, rs_out, rs_in, kacc, gainf, inv, rowacc, wbuf,
+    keys_ref, tg_hbm, wg_hbm, dsum_ref, wr,
+    tok, normed, u, wg, slab, cot, rs_out, rs_in, kacc, gainf, inv, rowacc, wbuf,
     d_in, d_own, d_send, d_parts, d_half, d_far, d_fin,
-    ss, rs, lsem, wsem,
+    ss, rs, lsem, wsem, osem,
 ):
     f32, bf16 = jnp.float32, jnp.bfloat16
     r, f = lax.axis_index("rep"), lax.axis_index("fsdp")
@@ -64,7 +68,7 @@
             src_ref=src, dst_ref=dst, send_sem=ss.at[ch], recv_sem=rs.at[ch], device_id=device
         )
 
-    sent = []
+    sent, written = [], []
 
     def send(ch, src, dst, device):
         cp = copy(ch, src, dst, device)
@@ -74,11 +78,10 @@
     def got(ch, dst):
         copy(ch, dst, dst, core).wait_recv()
 
-    own = pltpu.make_async_copy(kw.at[x, zh, c], wr.at[0, 0, c, 0], lsem.at[0])
     ldel = pltpu.make_async_copy(deltas.at[c], d_own, lsem.at[3])
     ltok = pltpu.make_async_copy(tok_hbm, tok, lsem.at[1])
     lcot = pltpu.make_async_copy(cot_hbm, cot.at[0], lsem.at[2])
-    for cp in (ldel, own, ltok, lcot):
+    for cp in (ldel, ltok, lcot):
         cp.start()
 
     barrier = pltpu.get_barrier_semaphore()
@@ -93,6 +96,8 @@
     send(E0, deltas.at[1 - c], d_in, core)
     for k in (1, 3, 2):
         send(A0 + k, kw.at[x, zh, c], wr.at[0, 0, c, 4 - k], dev(dy=k))
+    send(B0, kw.at[x, zh, c], wr.at[0, 3, c, 0], dev(dz=1))
+    send(K0, kw.at[x, zh, c], wr.at[0, 1, c, 0], dev(dz=3))
     for k in (1, 3, 2):
         send(C0 + k, cot_hbm, cot.at[4 - k], dev(dy=k))
 
@@ -110,7 +115,6 @@
     for k in (1, 3, 2):
         send(E0 + k, d_send.at[pl.ds(((x + k) % 4) * 2, 2)], d_parts.at[4 - k], dev(dx=k))
 
-    own.wait()
     for k in (1, 3, 2):
         got(A0 + k, wr.at[0, 0, c, 4 - k])
 
@@ -121,34 +125,49 @@
         lo, hi = SPAN[g]
         send(X0 + g, part(0, g, lo, hi), part(3, g, lo, hi), dev(dx=1))
         send(X0 + 4 + g, part(0, g, lo, hi), part(1, g, lo, hi), dev(dx=3))
+
+    def to_core(g):
+        lo, hi = SPAN[g]
         send(D0 + g, part(0, g, lo, hi), part(0, g, lo, hi), core)
 
     def forward(g):
         lo, hi = SPAN[g]
         got(X0 + g, part(3, g, lo, hi))
-        lo2, hi2 = FWD_P[g]
-        send(F0 + g, part(3, g, lo2, hi2), part(2, g, lo2, hi2), dev(dx=1))
+        if g % 2:
+            send(F0 + g, part(3, g, *FWD_P), part(2, g, *FWD_P), dev(dx=1))
         send(D0 + 4 + g, part(3, g, lo, hi), part(3, g, lo, hi), core)
         got(X0 + 4 + g, part(1, g, lo, hi))
-        lo2, hi2 = FWD_M[g]
-        send(F0 + 4 + g, part(1, g, lo2, hi2), part(2, g, lo2, hi2), dev(dx=3))
+        if g % 2:
+            send(F0 + 4 + g, part(1, g, *FWD_M), part(2, g, *FWD_M), dev(dx=3))
         send(D0 + 8 + g, part(1, g, lo, hi), part(1, g, lo, hi), core)
 
+    hi_dz = 3 - 2 * zl
+
     def swap(g):
-        for at, (lo, hi) in ((0, FWD_P[g]), (4, FWD_M[g])):
-            got(F0 + at + g, part(2, g, lo, hi))
-            send(D0 + 12 + at + g, part(2, g, lo, hi), part(2, g, lo, hi), core)
-
-    for k in (1, 3, 2):
-        lo, hi = SPAN[k]
-        send(B0 + k, part(0, 0, lo, hi), part(0, 4 - k, lo, hi), dev(dz=k))
+        got(F0 + g, part(2, g, *FWD_P))
+        got(F0 + 4 + g, part(2, g, *FWD_M))
+        send(H0 - 1 + g, part(2, g, 1, 4), part(2, (g + 4 - hi_dz) % 4, 1, 4), dev(dz=hi_dz))
+        send(D0 + 12 + g, part(2, g, 0, 4), part(2, g, 0, 4), core)
+
+    def across(g):
+        at = part(2, (g + hi_dz) % 4, 1, 4)
+        got(H0 - 1 + g, at)
+        send(D0 + 16 + g, at, at, core)
+
+    for k in (1, 3, 2):
+        send(B0 + k, part(0, 0, 1, 4), part(0, 4 - k, 1, 4), dev(dz=k))
     to_x(0)
+    to_core(0)
 
     def cols_of(i):
         return pl.ds(pl.multiple_of(i * CH, 128), CH)
 
     def fold(v):
         return v[:, :128] + v[:, 128:256] + v[:, 256:384]
+
+    def gain_of(col):
+        rows = [gainf[pl.ds(col // 128 + k, 1), :] for k in range(3)]
+        return jnp.concatenate(rows, axis=1)
 
     def wide(v):
         return jnp.concatenate([v, v, v], axis=1)
@@ -168,7 +187,7 @@
     @pl.loop(0, D // CH)
     def _(i):
         t = tok[:, cols_of(i)].astype(f32)
-        normed[:, cols_of(i)] = (t * wide(inv[...]) * gainf[:, cols_of(i)]).astype(bf16)
+        normed[:, cols_of(i)] = (t * wide(inv[...]) * gain_of(i * CH)).astype(bf16)
 
     rowacc[...] = jnp.zeros_like(rowacc)
     kacc[...] = jnp.zeros_like(kacc)
@@ -197,7 +216,10 @@
     def weight(j):
         total = product(4 + j)
         got(R0 + j, rs_in.at[j])
-        wg_ref[pl.ds(j * CH, CH), :] = (total + rs_in[j].astype(f32)).astype(bf16)
+        wg[j] = (total + rs_in[j].astype(f32)).astype(bf16)
+        cp = pltpu.make_async_copy(wg.at[j], wg_hbm.at[pl.ds(j * CH, CH)], osem.at[8 + j])
+        cp.start()
+        written.append(cp)
 
     block(0)
     block(1)
@@ -210,7 +232,7 @@
         up = lax.dot_general(
             cot[0], w, (((1,), (1,)), ((), ())), preferred_element_type=f32
         )
-        up = up * gainf[:, cols]
+        up = up * gain_of(col)
         rowacc[...] += fold(up * tok[:, cols].astype(f32))
         u[:, cols] = up * wide(inv[...])
 
@@ -259,8 +281,10 @@
 
     own_chunks()
     for g in (1, 3):
-        got(B0 + 4 - g, part(0, g, *SPAN[g]))
+        got(B0 if g == 3 else K0, part(0, g, 0, 1))
+        got(B0 + 4 - g, part(0, g, 1, 4))
         to_x(g)
+        to_core(g)
     forward(0)
 
     for k in (1, 3, 2):
@@ -284,20 +308,21 @@
     reduce(0)
     block(2)
     got(B0 + 2, part(0, 2, *SPAN[2]))
-    to_x(2)
+    to_core(2)
     reduce(1)
     block(3)
     for g in range(4):
         got_core(D0, 0, g, *SPAN[g])
+    chunks(0, 4, 4)
     forward(1)
     chunks(0, 1, 3)
     reduce(2)
     block(4)
-    chunks(0, 4, 4)
     forward(3)
+    to_x(2)
     reduce(3)
     block(5)
-    swap(0)
+    swap(1)
 
     got(G0, d_far)
 
@@ -310,56 +335,96 @@
 
     weight(0)
     block(6)
-    forward(2)
     for g in (1, 3):
         got_core(D0 + 4, 3, g, *SPAN[g])
         got_core(D0 + 8, 1, g, *SPAN[g])
     chunks(3, 4, 4)
+    swap(3)
     chunks(1, 4, 4)
     weight(1)
     block(7)
-    swap(1)
+    across(1)
+    got(G0 + 1, d_fin.at[1 - c])
+    for h in (0, 1):
+        turned = d_fin[h].T
+        dsum_ref[:, h * HALF:(h + 1) * HALF] = jnp.where(c == 1, turned[64:], turned[:64])
+    for g in (1, 3):
+        got_core(D0 + 12, 2, g, 0, 4)
+    chunks(2, 4, 4)
+    weight(2)
+    forward(2)
+    across(3)
     for g in (0, 2):
         got_core(D0 + 4, 3, g, *SPAN[g])
         got_core(D0 + 8, 1, g, *SPAN[g])
     chunks(3, 1, 3)
     chunks(1, 1, 3)
-    weight(2)
-    swap(3)
-    got(G0 + 1, d_fin.at[1 - c])
-    dsum_ref[...] = d_fin[...]
     for g in (1, 3):
-        got_core(D0 + 12, 2, g, *FWD_P[g])
-        got_core(D0 + 16, 2, g, *FWD_M[g])
-    chunks(2, 4, 4)
-    swap(2)
-    for g in (0, 2):
-        got_core(D0 + 12, 2, g, *FWD_P[g])
-        got_core(D0 + 16, 2, g, *FWD_M[g])
+        got(D0 + 16 + g, wr.at[2, (g + hi_dz) % 4, 1 - c, pl.ds(1, 3)])
     chunks(2, 1, 3)
     keys_ref[...] = kacc[...].astype(bf16)
 
     i1 = inv[...]
     inner = jnp.sum(rowacc[...], axis=1, keepdims=True) / D
     inv[...] = i1 * i1 * i1 * inner
-
-    def out(i):
-        cols = pl.ds(pl.multiple_of(i * SHARD, 128), SHARD)
-        return pltpu.make_async_copy(tok.at[:, cols], tg_hbm.at[:, cols], lsem.at[i])
-
     for i in range(8):
         @pl.loop(0, SHARD // CH)
         def _(j):
-            cols = pl.ds(pl.multiple_of(i * SHARD + j * CH, 128), CH)
+            cols = cols_of(i * (SHARD // CH) + j)
             t = tok[:, cols].astype(f32)
             tok[:, cols] = (u[:, cols] - t * wide(inv[...])).astype(bf16)
-        out(i).start()
-
+
+        cols = pl.ds(i * SHARD, SHARD)
+        cp = pltpu.make_async_copy(tok.at[:, cols], tg_hbm.at[:, cols], osem.at[i])
+        cp.start()
+        written.append(cp)
     weight(3)
-    for i in range(8):
-        out(i).wait()
+    for cp in written:
+        cp.wait()
     for cp in sent:
         cp.wait_send()
+
+
+def finish(
+    keys, tg, wg, dsum_hbm, anchor_hbm, momentum_hbm,
+    keys_out, tg_out, wg_out, anchor_out, momentum_out,
+    dsum, anchor, momentum, tg_here, wg_here, keys_here, sem, back,
+):
+    small = [
+        pltpu.make_async_copy(src, dst, sem.at[k])
+        for k, (src, dst) in enumerate(((dsum_hbm, dsum), (anchor_hbm, anchor), (momentum_hbm, momentum)))
+    ]
+    for cp in small:
+        cp.start()
+    moves = []
+    for src, here, dst, n in (
+        (tg, tg_here, tg_out, 8), (wg, wg_here, wg_out, 4), (keys, keys_here, keys_out, 1),
+    ):
+        step = src.shape[0] // n
+        for k in range(n):
+            rows, at = pl.ds(k * step, step), len(moves)
+            moves.append((
+                pltpu.make_async_copy(src.at[rows], here.at[rows], sem.at[3 + at]),
+                pltpu.make_async_copy(here.at[rows], dst.at[rows], back.at[2 + at]),
+            ))
+            moves[-1][0].start()
+    for come, go in moves:
+        come.wait()
+        go.start()
+    for cp in small:
+        cp.wait()
+    mean_delta = dsum[...] / 16
+    moved = OUTER_MU * momentum[...] + mean_delta
+    momentum[...] = moved
+    anchor[...] = anchor[...] - OUTER_LR * (mean_delta + OUTER_MU * moved)
+    last = [
+        pltpu.make_async_copy(anchor, anchor_out, back.at[0]),
+        pltpu.make_async_copy(momentum, momentum_out, back.at[1]),
+    ]
+    for cp in last:
+        cp.start()
+    for cp in [go for _, go in moves] + last:
+        cp.wait()
 
 
 def on_device(tokens, norm_gain, key_weight, cotangent, outer_deltas, anchor, momentum):
@@ -371,21 +436,22 @@
             jax.ShapeDtypeStruct((TOK, KW), bf16),
             jax.ShapeDtypeStruct((TOK, D), bf16),
             jax.ShapeDtypeStruct((SHARD, KW), bf16),
-            jax.ShapeDtypeStruct((2, HALF, 128), f32),
+            jax.ShapeDtypeStruct((64, SHARD), f32),
             jax.ShapeDtypeStruct((4, 4, 2, 4, PIECE, KW), bf16),
         ),
         in_specs=[any_space, vmem, any_space, any_space, any_space],
-        out_specs=(vmem, any_space, vmem, vmem, any_space),
+        out_specs=(vmem, any_space, any_space, vmem, any_space),
         scratch_shapes=[
             pltpu.VMEM((TOK, D), bf16),
             pltpu.VMEM((TOK, D), bf16),
             pltpu.VMEM((TOK, D), f32),
+            pltpu.VMEM((4, CH, KW), bf16),
             pltpu.VMEM((8, 4, TOK, CH), bf16),
             pltpu.VMEM((4, TOK, KW), bf16),
             pltpu.VMEM((4, CH, KW), bf16),
             pltpu.VMEM((4, CH, KW), bf16),
             pltpu.VMEM((TOK, KW), f32),
-            pltpu.VMEM((1, D), f32),
+            pltpu.VMEM((D // 128, 128), f32),
             pltpu.VMEM((TOK, 128), f32),
             pltpu.VMEM((TOK, 128), f32),
             pltpu.VMEM((2, 2, 2, PIECE, KW), bf16),
@@ -400,9 +466,10 @@
             pltpu.SemaphoreType.DMA((NCH,)),
             pltpu.SemaphoreType.DMA((8,)),
             pltpu.SemaphoreType.DMA((2, 2)),
+            pltpu.SemaphoreType.DMA((12,)),
         ],
         compiler_params=pltpu.CompilerParams(
-            collective_id=0, has_side_effects=True, vmem_limit_bytes=62 * 1024 * 1024
+            collective_id=0, has_side_effects=True, vmem_limit_bytes=LIMIT
         ),
         cost_estimate=pl.CostEstimate(
             flops=6 * TOK * D * KW, bytes_accessed=100_000_000, transcendentals=0
@@ -410,17 +477,34 @@
         name="step",
     )(
         tokens,
-        norm_gain.reshape(1, D),
+        norm_gain.reshape(D // 128, 128),
         key_weight.reshape(4, 2, 2, PIECE, KW),
         cotangent,
         outer_deltas.reshape(2, HALF, KW),
     )
-    delta_sum = delta_sum.reshape(SHARD, 128)
-    odd = lax.axis_index("rep") % 2 == 1
-    mean_delta = jnp.where(odd, delta_sum[:, 64:], delta_sum[:, :64]) / lax.axis_size("rep")
-    new_momentum = OUTER_MU * momentum + mean_delta
-    new_anchor = anchor - OUTER_LR * (mean_delta + OUTER_MU * new_momentum)
-    return (keys, token_grad, weight_grad[None], new_anchor, new_momentum)
+
+    keys, token_grad, weight_grad, new_anchor, new_momentum = pl.pallas_call(
+        finish,
+        out_shape=(
+            jax.ShapeDtypeStruct((TOK, KW), bf16),
+            jax.ShapeDtypeStruct((TOK, D), bf16),
+            jax.ShapeDtypeStruct((SHARD, KW), bf16),
+            jax.ShapeDtypeStruct((64, SHARD), f32),
+            jax.ShapeDtypeStruct((64, SHARD), f32),
+        ),
+        in_specs=[any_space] * 6,
+        out_specs=(any_space,) * 5,
+        scratch_shapes=[pltpu.VMEM((64, SHARD), f32)] * 3 + [
+            pltpu.VMEM((TOK, D), bf16),
+            pltpu.VMEM((SHARD, KW), bf16),
+            pltpu.VMEM((TOK, KW), bf16),
+            pltpu.SemaphoreType.DMA((16,)),
+            pltpu.SemaphoreType.DMA((15,)),
+        ],
+        compiler_params=pltpu.CompilerParams(vmem_limit_bytes=FINISH_LIMIT),
+        name="finish",
+    )(keys, token_grad, weight_grad, delta_sum, anchor.T, momentum.T)
+    return (keys, token_grad, weight_grad[None], new_anchor.T, new_momentum.T)
 
 
 def solution(mesh):

time: 150 us -> 141 us (0.940)
  local copies, waits for them, and re-layouts: 12.3 us -> 0 us
  Pallas kernels: 135 us -> 139 us
    unnamed x13 -> x0, local copies, waits for them, and re-layouts: 9.26 us -> none
    pallas_call x0 -> x1, Pallas kernels: none -> 8.28 us  [on_device(): pl.pallas_call(finish, out_shape=(jax.ShapeDtypeStruct((TOK, KW), bf16),...]
    pallas_call x1, Pallas kernels: 135 us -> 131 us  [on_device(): pl.pallas_call(kernel, out_shape=(jax.ShapeDtypeStruct((TOK, KW), bf16),...]
    slice x1 -> x0, local copies, waits for them, and re-layouts: 1.7 us -> none  [on_device(): delta_sum[:, :64]]
where the time goes in v3:
time: 141 us; the launch traced here: 140 us
  Pallas kernels  139 us (99%)
    pallas_call x1, Pallas kernels, on_device(): pl.pallas_call(kernel, out_shape=(jax.ShapeDtypeStruct((TOK, KW), bf16),...  131 us
    pallas_call x1, Pallas kernels, on_device(): pl.pallas_call(finish, out_shape=(jax.ShapeDtypeStruct((TOK, KW), bf16),...  8.28 us

profile of v3, /device:TPU:1, one launch (start us, length us, event | category | flops | bytes accessed | tf_op | source)
XLA Modules:
  0.0 139.9 jit_solution(15518076947137786179)
XLA Ops:
  0.6 131.0 %step.1 = (bf16[256,1024]{1,0:T(8,128)(2,1)}, bf16[256,12288]{1,0:T(8,128)(2,1)}, bf16[1536,1024]{1,0:T(8,128)(2,1)}, f32[64,1536]{1,0:T(8,128)}, bf16[4,4,2,4,96,1024]{5,4,3,2,1,0:T(8,128)(2,1)}) custom-call(bf16[256,12288]{1,0:T(8,128)(2,1)} %tok_hbm.1, bf16[96,128]{1,0:T(8,128)(2,1)} %bitcast.15, bf16[4,2,2,96,1024]{4,3,2,1,0:T(8,128)(2,1)} %bitcast.10, ...), custom_call_target="tpu_custom_call" | custom-call | flops 19327352832 | bytes 100000000 | tf_op jit(solution)/shard_map/step/pallas_call | solution.py:433
  131.6 8.3 %finish.1 = (bf16[256,1024]{1,0:T(8,128)(2,1)}, bf16[256,12288]{1,0:T(8,128)(2,1)}, bf16[1536,1024]{1,0:T(8,128)(2,1)}, f32[64,1536]{1,0:T(8,128)}, f32[64,1536]{1,0:T(8,128)}) custom-call(bf16[256,1024]{1,0:T(8,128)(2,1)} %get-tuple-element.14.keys, bf16[256,12288]{1,0:T(8,128)(2,1)} %get-tuple-element.15.tg, bf16[1536,1024]{1,0:T(8,128)(2,1)} %get-tuple-element.16.wg, ...), custom_call_target="tpu_custom_call" | custom-call | tf_op jit(solution)/shard_map/finish/pallas_call | solution.py:486

commit v4 on v3

--- a/solution.py
+++ b/solution.py
@@ -31,7 +31,8 @@
 R0 = 54
 T0 = 58
 K0 = 90
-NCH = 91
+E1 = 91
+NCH = 92
 
 LIMIT = 57 * 1024 * 1024
 FINISH_LIMIT = 58 * 1024 * 1024
@@ -44,7 +45,7 @@
     tok_hbm, gain_ref, kw, cot_hbm, deltas,
     keys_ref, tg_hbm, wg_hbm, dsum_ref, wr,
     tok, normed, u, wg, slab, cot, rs_out, rs_in, kacc, gainf, inv, rowacc, wbuf,
-    d_in, d_own, d_send, d_parts, d_half, d_far, d_fin,
+    d_in, d_own, d_send, d_relay, d_parts, d_half, d_far, d_fin,
     ss, rs, lsem, wsem, osem,
 ):
     f32, bf16 = jnp.float32, jnp.bfloat16
@@ -98,8 +99,6 @@
         send(A0 + k, kw.at[x, zh, c], wr.at[0, 0, c, 4 - k], dev(dy=k))
     send(B0, kw.at[x, zh, c], wr.at[0, 3, c, 0], dev(dz=1))
     send(K0, kw.at[x, zh, c], wr.at[0, 1, c, 0], dev(dz=3))
-    for k in (1, 3, 2):
-        send(C0 + k, cot_hbm, cot.at[4 - k], dev(dy=k))
 
     ldel.wait()
     got(E0, d_in)
@@ -112,8 +111,13 @@
             total = d_own[rows, cols].astype(f32) + d_in[rows, cols].astype(f32)
             d_send[q, rows, :] = total.astype(bf16)
 
-    for k in (1, 3, 2):
-        send(E0 + k, d_send.at[pl.ds(((x + k) % 4) * 2, 2)], d_parts.at[4 - k], dev(dx=k))
+    top, low = pl.ds(0, CH), pl.ds(CH, CH)
+
+    def pair(dx):
+        return pl.ds((x + dx) % 4 * 2, 2)
+
+    send(E0 + 1, d_send.at[pair(2), top], d_relay.at[0], dev(dx=1))
+    send(E0 + 2, d_send.at[pair(2), low], d_relay.at[1], dev(dx=3))
 
     for k in (1, 3, 2):
         got(A0 + k, wr.at[0, 0, c, 4 - k])
@@ -154,10 +158,29 @@
         got(H0 - 1 + g, at)
         send(D0 + 16 + g, at, at, core)
 
+    for k in (1, 3):
+        send(B0 + k, part(0, 0, 1, 4), part(0, 4 - k, 1, 4), dev(dz=k))
     for k in (1, 3, 2):
-        send(B0 + k, part(0, 0, 1, 4), part(0, 4 - k, 1, 4), dev(dz=k))
+        send(C0 + k, cot_hbm, cot.at[4 - k], dev(dy=k))
+    to_core(0)
+
+    def add_relay(at, dx, start):
+        @pl.loop(0, CH // 64)
+        def _(i):
+            here = pl.ds(pl.multiple_of(i * 64, 64), 64)
+            rows = pl.ds(pl.multiple_of(start + i * 64, 64), 64)
+            for h in (0, 1):
+                q = (x + dx) % 4 * 2 + h
+                total = d_send[q, rows, :].astype(f32) + d_relay[at, h, here, :].astype(f32)
+                d_send[q, rows, :] = total.astype(bf16)
+
+    got(E0 + 1, d_relay.at[0])
+    add_relay(0, 1, 0)
+    send(E0 + 3, d_send.at[pair(1)], d_parts.at[0], dev(dx=1))
+    got(E0 + 2, d_relay.at[1])
+    add_relay(1, 3, CH)
+    send(E1, d_send.at[pair(3)], d_parts.at[1], dev(dx=3))
     to_x(0)
-    to_core(0)
 
     def cols_of(i):
         return pl.ds(pl.multiple_of(i * CH, 128), CH)
@@ -222,7 +245,6 @@
         written.append(cp)
 
     block(0)
-    block(1)
     lcot.wait()
 
     def chunk(slot, col):
@@ -285,14 +307,15 @@
         got(B0 + 4 - g, part(0, g, 1, 4))
         to_x(g)
         to_core(g)
+    send(B0 + 2, part(0, 0, 1, 4), part(0, 2, 1, 4), dev(dz=2))
     forward(0)
 
-    for k in (1, 3, 2):
-        got(E0 + k, d_parts.at[4 - k])
+    got(E0 + 3, d_parts.at[0])
+    got(E1, d_parts.at[1])
 
     def over_x(half, rows):
         total = d_send[x * 2 + half, rows, :].astype(f32)
-        for k in (1, 2, 3):
+        for k in (0, 1):
             total = total + d_parts[k, half, rows, :].astype(f32)
         return total
 
@@ -305,6 +328,7 @@
 
     for k in (1, 3, 2):
         got(C0 + k, cot.at[4 - k])
+    block(1)
     reduce(0)
     block(2)
     got(B0 + 2, part(0, 2, *SPAN[2]))
@@ -351,13 +375,12 @@
     for g in (1, 3):
         got_core(D0 + 12, 2, g, 0, 4)
     chunks(2, 4, 4)
-    weight(2)
     forward(2)
-    across(3)
     for g in (0, 2):
         got_core(D0 + 4, 3, g, *SPAN[g])
         got_core(D0 + 8, 1, g, *SPAN[g])
     chunks(3, 1, 3)
+    across(3)
     chunks(1, 1, 3)
     for g in (1, 3):
         got(D0 + 16 + g, wr.at[2, (g + hi_dz) % 4, 1 - c, pl.ds(1, 3)])
@@ -378,6 +401,7 @@
         cp = pltpu.make_async_copy(tok.at[:, cols], tg_hbm.at[:, cols], osem.at[i])
         cp.start()
         written.append(cp)
+    weight(2)
     weight(3)
     for cp in written:
         cp.wait()
@@ -458,7 +482,8 @@
             pltpu.VMEM((HALF, KW), bf16),
             pltpu.VMEM((HALF, KW), bf16),
             pltpu.VMEM((8, HALF, 128), bf16),
-            pltpu.VMEM((4, 2, HALF, 128), bf16),
+            pltpu.VMEM((2, 2, CH, 128), bf16),
+            pltpu.VMEM((2, 2, HALF, 128), bf16),
             pltpu.VMEM((HALF, 128), bf16),
             pltpu.VMEM((HALF, 128), bf16),
             pltpu.VMEM((2, HALF, 128), f32),

time: 141 us -> 139 us (0.986)
    pallas_call x1, Pallas kernels: 131 us -> 129 us  [on_device(): pl.pallas_call(kernel, out_shape=(jax.ShapeDtypeStruct((TOK, KW), bf16),...]
where the time goes in v4:
time: 139 us
  Pallas kernels  138 us (99%)
    pallas_call x1, Pallas kernels, on_device(): pl.pallas_call(kernel, out_shape=(jax.ShapeDtypeStruct((TOK, KW), bf16),...  129 us
    pallas_call x1, Pallas kernels, on_device(): pl.pallas_call(finish, out_shape=(jax.ShapeDtypeStruct((TOK, KW), bf16),...  8.28 us

profile of v4, /device:TPU:1, one launch (start us, length us, event | category | flops | bytes accessed | tf_op | source)
XLA Modules:
  0.0 138.5 jit_solution(7064715693181669539)
XLA Ops:
  0.6 129.4 %step.1 = (bf16[256,1024]{1,0:T(8,128)(2,1)}, bf16[256,12288]{1,0:T(8,128)(2,1)}, bf16[1536,1024]{1,0:T(8,128)(2,1)}, f32[64,1536]{1,0:T(8,128)}, bf16[4,4,2,4,96,1024]{5,4,3,2,1,0:T(8,128)(2,1)}) custom-call(bf16[256,12288]{1,0:T(8,128)(2,1)} %tok_hbm.1, bf16[96,128]{1,0:T(8,128)(2,1)} %bitcast.15, bf16[4,2,2,96,1024]{4,3,2,1,0:T(8,128)(2,1)} %bitcast.10, ...), custom_call_target="tpu_custom_call" | custom-call | flops 19327352832 | bytes 100000000 | tf_op jit(solution)/shard_map/step/pallas_call | solution.py:457
  130.1 8.3 %finish.1 = (bf16[256,1024]{1,0:T(8,128)(2,1)}, bf16[256,12288]{1,0:T(8,128)(2,1)}, bf16[1536,1024]{1,0:T(8,128)(2,1)}, f32[64,1536]{1,0:T(8,128)}, f32[64,1536]{1,0:T(8,128)}) custom-call(bf16[256,1024]{1,0:T(8,128)(2,1)} %get-tuple-element.14.keys, bf16[256,12288]{1,0:T(8,128)(2,1)} %get-tuple-element.15.tg, bf16[1536,1024]{1,0:T(8,128)(2,1)} %get-tuple-element.16.wg, ...), custom_call_target="tpu_custom_call" | custom-call | tf_op jit(solution)/shard_map/finish/pallas_call | solution.py:511

commit v5 on v4

--- a/solution.py
+++ b/solution.py
@@ -32,13 +32,14 @@
 T0 = 58
 K0 = 90
 E1 = 91
-NCH = 92
+M0 = 92
+H1 = 100
+NCH = 104
 
 LIMIT = 57 * 1024 * 1024
 FINISH_LIMIT = 58 * 1024 * 1024
 
 SPAN = ((1, 4), (0, 4), (1, 4), (0, 4))
-FWD_P, FWD_M = (0, 2), (2, 4)
 
 
 def kernel(
@@ -103,21 +104,26 @@
     ldel.wait()
     got(E0, d_in)
 
-    @pl.loop(0, HALF // 32)
-    def _(i):
-        rows = pl.ds(pl.multiple_of(i * 32, 32), 32)
-        for q in range(8):
-            cols = slice(q * 128, (q + 1) * 128)
-            total = d_own[rows, cols].astype(f32) + d_in[rows, cols].astype(f32)
-            d_send[q, rows, :] = total.astype(bf16)
+    def both(steps):
+        @pl.loop(0, HALF // 64)
+        def _(i):
+            rows = pl.ds(pl.multiple_of(i * 64, 64), 64)
+            for dx in steps:
+                for h in (0, 1):
+                    q = (x + dx) % 4 * 2 + h
+                    cols = pl.ds(pl.multiple_of(q * 128, 128), 128)
+                    total = d_own[rows, cols].astype(f32) + d_in[rows, cols].astype(f32)
+                    d_send[q, rows, :] = total.astype(bf16)
 
     top, low = pl.ds(0, CH), pl.ds(CH, CH)
 
     def pair(dx):
         return pl.ds((x + dx) % 4 * 2, 2)
 
+    both((2,))
     send(E0 + 1, d_send.at[pair(2), top], d_relay.at[0], dev(dx=1))
     send(E0 + 2, d_send.at[pair(2), low], d_relay.at[1], dev(dx=3))
+    both((1, 3, 0))
 
     for k in (1, 3, 2):
         got(A0 + k, wr.at[0, 0, c, 4 - k])
@@ -138,24 +144,32 @@
         lo, hi = SPAN[g]
         got(X0 + g, part(3, g, lo, hi))
         if g % 2:
-            send(F0 + g, part(3, g, *FWD_P), part(2, g, *FWD_P), dev(dx=1))
+            send(F0 + g, part(3, g, 1, 2), part(2, g, 1, 2), dev(dx=1))
+            send(M0 + g, part(3, g, 0, 1), part(2, g, 0, 1), dev(dx=1))
         send(D0 + 4 + g, part(3, g, lo, hi), part(3, g, lo, hi), core)
         got(X0 + 4 + g, part(1, g, lo, hi))
         if g % 2:
-            send(F0 + 4 + g, part(1, g, *FWD_M), part(2, g, *FWD_M), dev(dx=3))
+            send(F0 + 4 + g, part(1, g, 2, 3), part(2, g, 2, 3), dev(dx=3))
+            send(M0 + 4 + g, part(1, g, 3, 4), part(2, g, 3, 4), dev(dx=3))
         send(D0 + 8 + g, part(1, g, lo, hi), part(1, g, lo, hi), core)
 
     hi_dz = 3 - 2 * zl
 
     def swap(g):
-        got(F0 + g, part(2, g, *FWD_P))
-        got(F0 + 4 + g, part(2, g, *FWD_M))
-        send(H0 - 1 + g, part(2, g, 1, 4), part(2, (g + 4 - hi_dz) % 4, 1, 4), dev(dz=hi_dz))
+        there = (g + 4 - hi_dz) % 4
+        got(F0 + g, part(2, g, 1, 2))
+        got(F0 + 4 + g, part(2, g, 2, 3))
+        send(H0 - 1 + g, part(2, g, 1, 3), part(2, there, 1, 3), dev(dz=hi_dz))
+        got(M0 + 4 + g, part(2, g, 3, 4))
+        send(H1 - 1 + g, part(2, g, 3, 4), part(2, there, 3, 4), dev(dz=hi_dz))
+        got(M0 + g, part(2, g, 0, 1))
         send(D0 + 12 + g, part(2, g, 0, 4), part(2, g, 0, 4), core)
 
     def across(g):
-        at = part(2, (g + hi_dz) % 4, 1, 4)
-        got(H0 - 1 + g, at)
+        here = (g + hi_dz) % 4
+        at = part(2, here, 1, 4)
+        got(H0 - 1 + g, part(2, here, 1, 3))
+        got(H1 - 1 + g, part(2, here, 3, 4))
         send(D0 + 16 + g, at, at, core)
 
     for k in (1, 3):
@@ -301,13 +315,13 @@
     def got_core(base, xrel, g, lo, hi):
         got(base + g, wr.at[xrel, g, 1 - c, pl.ds(lo, hi - lo)])
 
-    own_chunks()
     for g in (1, 3):
         got(B0 if g == 3 else K0, part(0, g, 0, 1))
         got(B0 + 4 - g, part(0, g, 1, 4))
         to_x(g)
         to_core(g)
     send(B0 + 2, part(0, 0, 1, 4), part(0, 2, 1, 4), dev(dz=2))
+    own_chunks()
     forward(0)
 
     got(E0 + 3, d_parts.at[0])

time: 139 us -> 138 us (level)
  no operation moved by 1% of the time
where the time goes in v5:
time: 138 us; the launch traced here: 137 us
  Pallas kernels  137 us (99%)
    pallas_call x1, Pallas kernels, on_device(): pl.pallas_call(kernel, out_shape=(jax.ShapeDtypeStruct((TOK, KW), bf16),...  128 us
    pallas_call x1, Pallas kernels, on_device(): pl.pallas_call(finish, out_shape=(jax.ShapeDtypeStruct((TOK, KW), bf16),...  8.28 us

profile of v5, /device:TPU:1, one launch (start us, length us, event | category | flops | bytes accessed | tf_op | source)
XLA Modules:
  0.0 137.3 jit_solution(12005389594514802689)
XLA Ops:
  0.6 128.2 %step.1 = (bf16[256,1024]{1,0:T(8,128)(2,1)}, bf16[256,12288]{1,0:T(8,128)(2,1)}, bf16[1536,1024]{1,0:T(8,128)(2,1)}, f32[64,1536]{1,0:T(8,128)}, bf16[4,4,2,4,96,1024]{5,4,3,2,1,0:T(8,128)(2,1)}) custom-call(bf16[256,12288]{1,0:T(8,128)(2,1)} %tok_hbm.1, bf16[96,128]{1,0:T(8,128)(2,1)} %bitcast.15, bf16[4,2,2,96,1024]{4,3,2,1,0:T(8,128)(2,1)} %bitcast.10, ...), custom_call_target="tpu_custom_call" | custom-call | flops 19327352832 | bytes 100000000 | tf_op jit(solution)/shard_map/step/pallas_call | solution.py:471
  128.9 8.3 %finish.1 = (bf16[256,1024]{1,0:T(8,128)(2,1)}, bf16[256,12288]{1,0:T(8,128)(2,1)}, bf16[1536,1024]{1,0:T(8,128)(2,1)}, f32[64,1536]{1,0:T(8,128)}, f32[64,1536]{1,0:T(8,128)}) custom-call(bf16[256,1024]{1,0:T(8,128)(2,1)} %get-tuple-element.14.keys, bf16[256,12288]{1,0:T(8,128)(2,1)} %get-tuple-element.15.tg, bf16[1536,1024]{1,0:T(8,128)(2,1)} %get-tuple-element.16.wg, ...), custom_call_target="tpu_custom_call" | custom-call | tf_op jit(solution)/shard_map/finish/pallas_call | solution.py:525

commit v6 on v5

--- a/solution.py
+++ b/solution.py
@@ -36,7 +36,7 @@
 H1 = 100
 NCH = 104
 
-LIMIT = 57 * 1024 * 1024
+LIMIT = 59 * 1024 * 1024
 FINISH_LIMIT = 58 * 1024 * 1024
 
 SPAN = ((1, 4), (0, 4), (1, 4), (0, 4))
@@ -45,7 +45,7 @@
 def kernel(
     tok_hbm, gain_ref, kw, cot_hbm, deltas,
     keys_ref, tg_hbm, wg_hbm, dsum_ref, wr,
-    tok, normed, u, wg, slab, cot, rs_out, rs_in, kacc, gainf, inv, rowacc, wbuf,
+    tok, normed, u, wg, early, slab, cot, rs_out, rs_in, kacc, gainf, inv, rowacc, wbuf,
     d_in, d_own, d_send, d_relay, d_parts, d_half, d_far, d_fin,
     ss, rs, lsem, wsem, osem,
 ):
@@ -251,7 +251,7 @@
         send(R0 + j, rs_out.at[j], rs_in.at[j], beside)
 
     def weight(j):
-        total = product(4 + j)
+        total = early[...] if j == 2 else product(4 + j)
         got(R0 + j, rs_in.at[j])
         wg[j] = (total + rs_in[j].astype(f32)).astype(bf16)
         cp = pltpu.make_async_copy(wg.at[j], wg_hbm.at[pl.ds(j * CH, CH)], osem.at[8 + j])
@@ -389,6 +389,7 @@
     for g in (1, 3):
         got_core(D0 + 12, 2, g, 0, 4)
     chunks(2, 4, 4)
+    early[...] = product(6)
     forward(2)
     for g in (0, 2):
         got_core(D0 + 4, 3, g, *SPAN[g])
@@ -484,6 +485,7 @@
             pltpu.VMEM((TOK, D), bf16),
             pltpu.VMEM((TOK, D), f32),
             pltpu.VMEM((4, CH, KW), bf16),
+            pltpu.VMEM((CH, KW), f32),
             pltpu.VMEM((8, 4, TOK, CH), bf16),
             pltpu.VMEM((4, TOK, KW), bf16),
             pltpu.VMEM((4, CH, KW), bf16),

time: 138 us -> 137 us (level)
  no operation moved by 1% of the time
where the time goes in v6:
time: 137 us
  Pallas kernels  136 us (99%)
    pallas_call x1, Pallas kernels, on_device(): pl.pallas_call(kernel, out_shape=(jax.ShapeDtypeStruct((TOK, KW), bf16),...  128 us
    pallas_call x1, Pallas kernels, on_device(): pl.pallas_call(finish, out_shape=(jax.ShapeDtypeStruct((TOK, KW), bf16),...  8.28 us

profile of v6, /device:TPU:1, one launch (start us, length us, event | category | flops | bytes accessed | tf_op | source)
XLA Modules:
  0.0 136.7 jit_solution(5602730900319749218)
XLA Ops:
  0.6 127.8 %step.1 = (bf16[256,1024]{1,0:T(8,128)(2,1)}, bf16[256,12288]{1,0:T(8,128)(2,1)}, bf16[1536,1024]{1,0:T(8,128)(2,1)}, f32[64,1536]{1,0:T(8,128)}, bf16[4,4,2,4,96,1024]{5,4,3,2,1,0:T(8,128)(2,1)}) custom-call(bf16[256,12288]{1,0:T(8,128)(2,1)} %tok_hbm.1, bf16[96,128]{1,0:T(8,128)(2,1)} %bitcast.15, bf16[4,2,2,96,1024]{4,3,2,1,0:T(8,128)(2,1)} %bitcast.10, ...), custom_call_target="tpu_custom_call" | custom-call | flops 19327352832 | bytes 100000000 | tf_op jit(solution)/shard_map/step/pallas_call | solution.py:472
  128.4 8.3 %finish.1 = (bf16[256,1024]{1,0:T(8,128)(2,1)}, bf16[256,12288]{1,0:T(8,128)(2,1)}, bf16[1536,1024]{1,0:T(8,128)(2,1)}, f32[64,1536]{1,0:T(8,128)}, f32[64,1536]{1,0:T(8,128)}) custom-call(bf16[256,1024]{1,0:T(8,128)(2,1)} %get-tuple-element.14.keys, bf16[256,12288]{1,0:T(8,128)(2,1)} %get-tuple-element.15.tg, bf16[1536,1024]{1,0:T(8,128)(2,1)} %get-tuple-element.16.wg, ...), custom_call_target="tpu_custom_call" | custom-call | tf_op jit(solution)/shard_map/finish/pallas_call | solution.py:527
